TPU v7x, 32 devices: a whole 2x2x4 slice. The times are simulated.
32 devices in a mesh: slab: 2 (over x), brick: 16 (over z, y, core).
Axes of the slice: x: 2, y: 2, z: 4, core: 2. Of those that a mesh axis runs over, the one named last changes fastest.
Arguments:
- features: bfloat16 [64, 64, 512], P(('slab', 'brick')), may hold values from -6 to 6
- weight: bfloat16 [27, 64, 64], replicated, may hold values from -0.15625 to 0.15625
- cotangent: bfloat16 [64, 64, 512], P(('slab', 'brick')), may hold values from -6 to 6
- occupancy: int32 [64, 24], P(('slab', 'brick')), may hold values from 0 to 4194303, as said below
- neighbours: int32 [64, 27], P(('slab', 'brick')), may hold values from -1 to 63, as said below
Outputs:
- output: bfloat16 [64, 64, 512], P(('slab', 'brick'))
- grad_input: bfloat16 [64, 64, 512], P(('slab', 'brick'))
- grad_weight: float32 [27, 64, 64], replicated
Inputs may be any that keep to these rules, and one draw needn't show every extreme that they name: `neighbours`: slot j of the device at (slab s, brick t), that is slot (16 s + t) * 2 + j, holds the brick of z layer 2 s + j and column t along x, at some row y; slot 0 of every device holds a brick, the others may be absent. For offset k = 9 (a + 1) + 3 (c + 1) + (e + 1), the entry of a present slot is the slot that holds the brick at layer 2 s + j + a, row y + c, column t + e if that brick is present, else -1; an absent slot's entries are all -1. The lists are symmetric, and the middle entry of a present slot is the slot itself. Bit j of word w of a slot is the occupancy of voxel 22 w + j; bits from voxel 512 on are zero. Absent slots are wholly unoccupied; slot 0 is fully occupied.
All inputs are finite; a program needn't handle non-finite values.
Results may differ from a plain program's by a relative error of at most 0.001.
Values may be sent and summed in bfloat16 or wider, within the bound.
A program may use at most 64 MiB of HBM per device.

v0:
```python
import math
import jax
import jax.numpy as jnp
from jax import lax
from jax.sharding import PartitionSpec as P

EDGE = 8


def extended(block, sides, width):
    for axis, dim in sides:
        count = lax.axis_size(axis)
        forward = [(i, i + 1) for i in range(count - 1)]
        backward = [(target, source) for source, target in forward]
        low = lax.ppermute(
            lax.slice_in_dim(block, block.shape[dim] - width, None, axis=dim), axis, forward
        )
        high = lax.ppermute(lax.slice_in_dim(block, 0, width, axis=dim), axis, backward)
        block = jnp.concatenate([low, block, high], axis=dim)
    return block


def unpack_bits(packed, voxels):
    places = jnp.arange(22, dtype=jnp.int32)
    bit_table = jnp.bitwise_and(jnp.right_shift(packed[..., :, None], places), 1)
    return bit_table.reshape(packed.shape[:-1] + (packed.shape[-1] * 22,))[..., :voxels]


def cut(length, side):
    if side < 0:
        return slice(length - 1, length)
    if side > 0:
        return slice(0, 1)
    return slice(0, length)


def windows(padded, direction):
    channels = padded.shape[0]
    pieces = []
    for shift_z in (-1, 0, 1):
        for shift_y in (-1, 0, 1):
            for shift_x in (-1, 0, 1):
                begin_z = 1 + direction * shift_z
                begin_y = 1 + direction * shift_y
                begin_x = 1 + direction * shift_x
                window = padded[
                    :, begin_z : begin_z + EDGE, begin_y : begin_y + EDGE, begin_x : begin_x + EDGE
                ]
                pieces.append(window.reshape(channels, EDGE * EDGE * EDGE))
    return jnp.stack(pieces, 0).reshape(27 * channels, EDGE * EDGE * EDGE)


def first_row(face):
    return face.reshape(face.shape[0], EDGE, EDGE)[:, 0, :]


def last_row(face):
    return face.reshape(face.shape[0], EDGE, EDGE)[:, EDGE - 1, :]


def per_device(features, weight, cotangent, occupancy, neighbours):
    slots = features.shape[0]
    channels = features.shape[1]
    voxels = features.shape[2]
    width = 2 * channels
    face_size = EDGE * EDGE
    occupied = unpack_bits(occupancy, voxels).astype(jnp.bfloat16)
    masked_input = features * occupied[:, None, :]
    masked_grad = cotangent * occupied[:, None, :]
    cube = jnp.concatenate([masked_input, masked_grad], 1).reshape(slots, width, EDGE, EDGE, EDGE)
    present = (neighbours >= 0).astype(jnp.bfloat16)
    low_x = cube[..., 0].reshape(slots, width, face_size)
    high_x = cube[..., EDGE - 1].reshape(slots, width, face_size)
    low_z = cube[0, :, 0].reshape(width, face_size)
    high_z = cube[slots - 1, :, EDGE - 1].reshape(width, face_size)
    payload = jnp.concatenate([low_x, high_x, low_z[None], high_z[None]], 0)
    beside_all = extended(payload[None, None], (("slab", 0), ("brick", 1)), 1)
    right_faces = beside_all[1, 2, :slots]
    left_faces = beside_all[1, 0, slots : 2 * slots]
    above_face = beside_all[2, 1, 2 * slots]
    below_face = beside_all[0, 1, 2 * slots + 1]
    above_right = first_row(beside_all[2, 2, 0])
    above_left = first_row(beside_all[2, 0, slots])
    below_right = last_row(beside_all[0, 2, slots - 1])
    below_left = last_row(beside_all[0, 0, 2 * slots - 1])

    def piece(slot, shift_z, shift_y, shift_x):
        target = slot + shift_z
        offset = 9 * (shift_z + 1) + 3 * (shift_y + 1) + (shift_x + 1)
        span_z = cut(EDGE, shift_z)
        span_y = cut(EDGE, shift_y)
        if 0 <= target < slots:
            if shift_x == 0:
                block = cube[target][:, span_z, span_y, :]
            else:
                source = right_faces if shift_x == 1 else left_faces
                block = source[target].reshape(width, EDGE, EDGE)[:, span_z, span_y][..., None]
        elif target >= slots:
            if shift_x == 0:
                block = above_face.reshape(width, EDGE, EDGE)[:, None, span_y, :]
            else:
                edge_row = above_right if shift_x == 1 else above_left
                block = edge_row[:, None, span_y, None]
        elif shift_x == 0:
            block = below_face.reshape(width, EDGE, EDGE)[:, None, span_y, :]
        else:
            edge_row = below_right if shift_x == 1 else below_left
            block = edge_row[:, None, span_y, None]
        return block * present[slot, offset]

    forward_matrix = jnp.transpose(weight, (1, 0, 2)).reshape(channels, 27 * channels)
    backward_matrix = jnp.transpose(weight, (2, 0, 1)).reshape(channels, 27 * channels)
    outputs = []
    gradients = []
    local_terms = jnp.zeros((channels, 27 * channels), jnp.float32)
    for slot in range(slots):
        layers = []
        for shift_z in (-1, 0, 1):
            rows = []
            for shift_y in (-1, 0, 1):
                columns = [piece(slot, shift_z, shift_y, shift_x) for shift_x in (-1, 0, 1)]
                rows.append(jnp.concatenate(columns, 3))
            layers.append(jnp.concatenate(rows, 2))
        padded = jnp.concatenate(layers, 1)
        scaling = occupied[slot].astype(jnp.float32)[None, :]
        input_patches = windows(padded[:channels], 1)
        output_rows = jnp.dot(forward_matrix, input_patches, preferred_element_type=jnp.float32)
        outputs.append((output_rows * scaling).astype(jnp.bfloat16))
        local_terms = local_terms + lax.dot_general(
            masked_grad[slot],
            input_patches,
            (((1,), (1,)), ((), ())),
            preferred_element_type=jnp.float32,
        )
        grad_patches = windows(padded[channels:], -1)
        grad_rows = jnp.dot(backward_matrix, grad_patches, preferred_element_type=jnp.float32)
        gradients.append((grad_rows * scaling).astype(jnp.bfloat16))
    total = lax.psum(local_terms, ("slab", "brick"))
    slot_count = slots * lax.axis_size("slab") * lax.axis_size("brick")
    grad_weight = jnp.transpose(total.reshape(channels, 27, channels), (1, 0, 2)) / math.sqrt(
        voxels * slot_count
    )
    return (jnp.stack(outputs, 0), jnp.stack(gradients, 0), grad_weight)


def solution(mesh):
    placed = (
        P(("slab", "brick"), None, None),
        P(),
        P(("slab", "brick"), None, None),
        P(("slab", "brick"), None),
        P(("slab", "brick"), None),
    )
    return jax.shard_map(
        per_device,
        mesh=mesh,
        in_specs=placed,
        out_specs=(P(("slab", "brick"), None, None), P(("slab", "brick"), None, None), P()),
        check_vma=False,
    )
```

profile of v0, /device:TPU:1, one launch (start us, length us, event | category | flops | bytes accessed | tf_op | source)
XLA Modules:
  0.0 351.3 jit_solution(4987366351810817979)
XLA Ops:
  12.2 4.0 %collective-permute-start = (bf16[1,1,6,128,64]{3,4,2,1,0:T(8,128)(2,1)S(1)}, bf16[1,1,6,128,64]{3,4,2,1,0:T(8,128)(2,1)S(1)}, u32[]{:S(2)}, u32[]{:S(2)}) collective-permute-start(bf16[1,1,6,128,64]{3,4,2,1,0:T(8,128)(2,1)S(1)} %maximum_bitcast_fusion), channel_id=1, source_target_pairs={{0,16},{1,17},{2,18},{3,19},{4,20},{5,21},{6,22},{7,23},{8,24},{9,... | collective-permute-start | bytes 294920 | tf_op jit(solution)/shard_map/ppermute | solution.py:15
  22.9 1.9 slice_multiply_fusion.19
  27.4 1.8 slice_multiply_fusion.15
  29.3 2.8 collective-permute-start.3
  32.1 4.2 %collective-permute-start.2 = (bf16[3,1,6,128,64]{3,4,2,1,0:T(8,128)(2,1)S(1)}, bf16[3,1,6,128,64]{3,4,2,1,0:T(8,128)(2,1)S(1)}, u32[]{:S(2)}, u32[]{:S(2)}) collective-permute-start(bf16[3,1,6,128,64]{3,4,2,1,0:T(8,128)(2,1)S(1)} %pad_maximum_fusion), channel_id=1, source_target_pairs={{0,1},{1,2},{2,3},{3,4},{4,5},{5,6},{6,7},{7,8},{8,9},{9,10},{10,1... | collective-permute-start | bytes 884744 | tf_op jit(solution)/shard_map/ppermute | solution.py:15
  38.7 1.8 fusion.28
  40.5 1.9 fusion.34
  69.4 1.6 copy.308
  71.0 1.6 copy.307
  72.7 1.6 copy.306
  74.3 1.6 copy.259
  111.3 2.0 fusion.45
  113.3 2.0 fusion.46
  115.6 1.6 fusion.48
  117.1 1.6 copy.277
  118.7 1.6 copy.276
  120.4 1.6 copy.275
  122.0 1.6 copy.274
  123.6 1.6 copy.273
  125.2 1.6 copy.272
  126.8 1.6 copy.271
  128.5 1.6 copy.270
  130.1 1.6 copy.269
  131.7 1.6 copy.229
  133.3 1.6 copy.228
  134.9 1.7 copy.227
  154.0 2.1 fusion.41
  156.1 1.9 fusion.42
  159.8 1.6 copy.323
  161.4 1.6 copy.322
  176.8 1.6 fusion.50
  178.4 1.6 copy.305
  180.0 1.6 copy.304
  181.6 1.6 copy.303
  183.2 1.6 copy.302
  184.9 1.6 copy.301
  186.5 1.6 copy.300
  188.1 1.6 copy.299
  189.7 1.6 copy.298
  191.4 1.6 copy.297
  193.0 1.6 copy.268
  194.6 1.6 copy.267
  196.2 1.6 copy.266
  197.9 1.6 copy.265
  199.5 1.6 copy.264
  213.8 1.4 convolution_add_fusion
  219.3 122.2 %all-reduce.2.cloned.1.call-done = f32[64,1728]{1,0:T(8,128)} async-done(((f32[64,1728]{1,0:T(8,128)}), f32[64,1728]{1,0:T(8,128)}) %all-reduce.2.cloned.1.call-update) | async-done | bytes 442384 | tf_op jit(solution)/shard_map/psum | solution.py:138
  343.0 1.4 copy.325
  (559 shorter events, 127.9 us)
Async XLA Ops:
  7.2 143.5 %copy-start = (bf16[27,64,64]{2,1,0:T(8,128)(2,1)S(1)}, bf16[27,64,64]{2,1,0:T(8,128)(2,1)}, u32[]{:S(2)}) copy-start(bf16[27,64,64]{2,1,0:T(8,128)(2,1)} %param.6) | copy-start | bytes 663556
  7.2 334.3 %all-reduce.2.cloned.1.call-start = ((), (), s32[]{:S(2)}) async-start(), calls=%async_computation | async-start | bytes 917504 | tf_op jit(solution)/shard_map/psum | solution.py:138
  10.9 18.3 %collective-permute-start.1 = (bf16[1,1,6,128,64]{3,4,2,1,0:T(8,128)(2,1)S(1)}, bf16[1,1,6,128,64]{3,4,2,1,0:T(8,128)(2,1)S(1)}, u32[]{:S(2)}, u32[]{:S(2)}) collective-permute-start(bf16[1,1,6,128,64]{3,4,2,1,0:T(8,128)(2,1)S(1)} %maximum_bitcast_fusion), channel_id=1, source_target_pairs={{16,0},{17,1},{18,2},{19,3},{20,4},{21,5},{22,6},{23,7},{24,8},{25... | collective-permute-start | bytes 294920 | tf_op jit(solution)/shard_map/ppermute | solution.py:18
  12.2 17.0 %collective-permute-start = (bf16[1,1,6,128,64]{3,4,2,1,0:T(8,128)(2,1)S(1)}, bf16[1,1,6,128,64]{3,4,2,1,0:T(8,128)(2,1)S(1)}, u32[]{:S(2)}, u32[]{:S(2)}) collective-permute-start(bf16[1,1,6,128,64]{3,4,2,1,0:T(8,128)(2,1)S(1)} %maximum_bitcast_fusion), channel_id=1, source_target_pairs={{0,16},{1,17},{2,18},{3,19},{4,20},{5,21},{6,22},{7,23},{8,24},{9,... | collective-permute-start | bytes 294920 | tf_op jit(solution)/shard_map/ppermute | solution.py:15
  27.4 33.3 %copy-start.86 = (bf16[128,8,1,8]{0,3,2,1:T(8,128)(2,1)}, bf16[128,8,1,8]{0,3,2,1:T(8,128)(2,1)S(1)}, u32[]{:S(2)}) copy-start(bf16[128,8,1,8]{0,3,2,1:T(8,128)(2,1)S(1)} %get-tuple-element.145) | copy-start | bytes 49156
  27.4 33.3 %copy-start.88 = (bf16[128,8,1,8]{0,3,2,1:T(8,128)(2,1)}, bf16[128,8,1,8]{0,3,2,1:T(8,128)(2,1)S(1)}, u32[]{:S(2)}) copy-start(bf16[128,8,1,8]{0,3,2,1:T(8,128)(2,1)S(1)} %get-tuple-element.146) | copy-start | bytes 49156
  29.3 13.1 %collective-permute-start.3 = (bf16[3,1,6,128,64]{3,4,2,1,0:T(8,128)(2,1)S(1)}, bf16[3,1,6,128,64]{3,4,2,1,0:T(8,128)(2,1)S(1)}, u32[]{:S(2)}, u32[]{:S(2)}) collective-permute-start(bf16[3,1,6,128,64]{3,4,2,1,0:T(8,128)(2,1)S(1)} %pad_maximum_fusion), channel_id=1, source_target_pairs={{1,0},{2,1},{3,2},{4,3},{5,4},{6,5},{7,6},{8,7},{9,8},{10,9},{11,1... | collective-permute-start | bytes 884744 | tf_op jit(solution)/shard_map/ppermute | solution.py:18
  32.1 18.9 %collective-permute-start.2 = (bf16[3,1,6,128,64]{3,4,2,1,0:T(8,128)(2,1)S(1)}, bf16[3,1,6,128,64]{3,4,2,1,0:T(8,128)(2,1)S(1)}, u32[]{:S(2)}, u32[]{:S(2)}) collective-permute-start(bf16[3,1,6,128,64]{3,4,2,1,0:T(8,128)(2,1)S(1)} %pad_maximum_fusion), channel_id=1, source_target_pairs={{0,1},{1,2},{2,3},{3,4},{4,5},{5,6},{6,7},{7,8},{8,9},{9,10},{10,1... | collective-permute-start | bytes 884744 | tf_op jit(solution)/shard_map/ppermute | solution.py:15
  43.6 21.7 %copy-start.116 = (bf16[128,8,8]{0,2,1:T(8,128)(2,1)}, bf16[128,8,8]{0,2,1:T(8,128)(2,1)S(1)}, u32[]{:S(2)}) copy-start(bf16[128,8,8]{0,2,1:T(8,128)(2,1)S(1)} %get-tuple-element.117) | copy-start | bytes 49156
  47.3 13.4 %copy-start.102 = (bf16[128,8,1,1]{0,3,2,1:T(2,128)(2,1)}, bf16[128,8,1,1]{0,3,2,1:T(2,128)(2,1)S(1)}, u32[]{:S(2)}) copy-start(bf16[128,8,1,1]{0,3,2,1:T(2,128)(2,1)S(1)} %copy.198) | copy-start | bytes 6148
  47.3 13.4 %copy-start.104 = (bf16[128,8,1,1]{0,3,2,1:T(2,128)(2,1)}, bf16[128,8,1,1]{0,3,2,1:T(2,128)(2,1)S(1)}, u32[]{:S(2)}) copy-start(bf16[128,8,1,1]{0,3,2,1:T(2,128)(2,1)S(1)} %copy.192) | copy-start | bytes 6148
  52.4 14.2 %copy-start.117 = (bf16[128,8,8]{0,2,1:T(8,128)(2,1)}, bf16[128,8,8]{0,2,1:T(8,128)(2,1)S(1)}, u32[]{:S(2)}) copy-start(bf16[128,8,8]{0,2,1:T(8,128)(2,1)S(1)} %get-tuple-element.111) | copy-start | bytes 49156
  87.7 10.1 %copy-start.103 = (bf16[128,8,1,1]{0,3,2,1:T(2,128)(2,1)S(1)}, bf16[128,8,1,1]{0,3,2,1:T(2,128)(2,1)}, u32[]{:S(2)}) copy-start(bf16[128,8,1,1]{0,3,2,1:T(2,128)(2,1)} %copy-done.102) | copy-start | bytes 6148
  87.8 10.1 %copy-start.105 = (bf16[128,8,1,1]{0,3,2,1:T(2,128)(2,1)S(1)}, bf16[128,8,1,1]{0,3,2,1:T(2,128)(2,1)}, u32[]{:S(2)}) copy-start(bf16[128,8,1,1]{0,3,2,1:T(2,128)(2,1)} %copy-done.104) | copy-start | bytes 6148
  87.8 10.1 %copy-start.107 = (bf16[128,8,1,1]{0,3,2,1:T(2,128)(2,1)S(1)}, bf16[128,8,1,1]{0,3,2,1:T(2,128)(2,1)}, u32[]{:S(2)}) copy-start(bf16[128,8,1,1]{0,3,2,1:T(2,128)(2,1)} %copy-done.106) | copy-start | bytes 6148
  87.8 10.1 %copy-start.109 = (bf16[128,8,1,1]{0,3,2,1:T(2,128)(2,1)S(1)}, bf16[128,8,1,1]{0,3,2,1:T(2,128)(2,1)}, u32[]{:S(2)}) copy-start(bf16[128,8,1,1]{0,3,2,1:T(2,128)(2,1)} %copy-done.108) | copy-start | bytes 6148
  87.8 10.1 %copy-start.111 = (bf16[128,1,8,8]{0,3,2,1:T(8,128)(2,1)S(1)}, bf16[128,1,8,8]{0,3,2,1:T(8,128)(2,1)}, u32[]{:S(2)}) copy-start(bf16[128,1,8,8]{0,3,2,1:T(8,128)(2,1)} %get-tuple-element.151) | copy-start | bytes 49156
  87.8 10.1 %copy-start.124 = (bf16[128,1,8,1]{0,3,2,1:T(2,128)(2,1)S(1)}, bf16[128,1,8,1]{0,3,2,1:T(2,128)(2,1)}, u32[]{:S(2)}) copy-start(bf16[128,1,8,1]{0,3,2,1:T(2,128)(2,1)} %copy.188) | copy-start | bytes 6148
  87.8 10.1 %copy-start.125 = (bf16[128,1,8,1]{0,3,2,1:T(2,128)(2,1)S(1)}, bf16[128,1,8,1]{0,3,2,1:T(2,128)(2,1)}, u32[]{:S(2)}) copy-start(bf16[128,1,8,1]{0,3,2,1:T(2,128)(2,1)} %copy.187) | copy-start | bytes 6148
  87.8 10.1 %copy-start.132 = (bf16[128,1,1,8]{0,3,2,1:T(8,128)(2,1)S(1)}, bf16[128,1,1,8]{0,3,2,1:T(8,128)(2,1)}, u32[]{:S(2)}) copy-start(bf16[128,1,1,8]{0,3,2,1:T(8,128)(2,1)} %get-tuple-element.159) | copy-start | bytes 6148
  99.5 15.7 %copy-start.113 = (bf16[128,1,8,8]{0,3,2,1:T(8,128)(2,1)S(1)}, bf16[128,1,8,8]{0,3,2,1:T(8,128)(2,1)}, u32[]{:S(2)}) copy-start(bf16[128,1,8,8]{0,3,2,1:T(8,128)(2,1)} %slice_multiply_fusion.3) | copy-start | bytes 49156
  99.5 15.7 %copy-start.122 = (bf16[128,1,8,1]{0,3,2,1:T(2,128)(2,1)S(1)}, bf16[128,1,8,1]{0,3,2,1:T(2,128)(2,1)}, u32[]{:S(2)}) copy-start(bf16[128,1,8,1]{0,3,2,1:T(2,128)(2,1)} %copy.202) | copy-start | bytes 6148
  99.5 15.7 %copy-start.123 = (bf16[128,1,8,1]{0,3,2,1:T(2,128)(2,1)S(1)}, bf16[128,1,8,1]{0,3,2,1:T(2,128)(2,1)}, u32[]{:S(2)}) copy-start(bf16[128,1,8,1]{0,3,2,1:T(2,128)(2,1)} %copy.201) | copy-start | bytes 6148
  99.6 15.7 %copy-start.130 = (bf16[128,1,1,8]{0,3,2,1:T(8,128)(2,1)S(1)}, bf16[128,1,1,8]{0,3,2,1:T(8,128)(2,1)}, u32[]{:S(2)}) copy-start(bf16[128,1,1,8]{0,3,2,1:T(8,128)(2,1)} %get-tuple-element.143) | copy-start | bytes 6148
  99.6 15.8 %copy-start.131 = (bf16[128,1,1,8]{0,3,2,1:T(8,128)(2,1)S(1)}, bf16[128,1,1,8]{0,3,2,1:T(8,128)(2,1)}, u32[]{:S(2)}) copy-start(bf16[128,1,1,8]{0,3,2,1:T(8,128)(2,1)} %get-tuple-element.144) | copy-start | bytes 6148
  134.9 14.7 %copy-start.20 = (bf16[1,64,512]{2,1,0:T(8,128)(2,1)S(1)}, bf16[1,64,512]{2,1,0:T(8,128)(2,1)}, u32[]{:S(2)}) copy-start(bf16[1,64,512]{2,1,0:T(8,128)(2,1)} %copy.220) | copy-start | bytes 196612
  137.3 12.2 %copy-start.24 = (bf16[1,64,512]{2,1,0:T(8,128)(2,1)S(1)}, bf16[1,64,512]{2,1,0:T(8,128)(2,1)}, u32[]{:S(2)}) copy-start(bf16[1,64,512]{2,1,0:T(8,128)(2,1)} %copy.218) | copy-start | bytes 196612
  137.3 12.3 %copy-start.23 = (bf16[1,64,512]{2,1,0:T(8,128)(2,1)S(1)}, bf16[1,64,512]{2,1,0:T(8,128)(2,1)}, u32[]{:S(2)}) copy-start(bf16[1,64,512]{2,1,0:T(8,128)(2,1)} %copy.219) | copy-start | bytes 196612
  138.0 11.4 %copy-start.42 = (bf16[1,64,512]{2,1,0:T(8,128)(2,1)S(1)}, bf16[1,64,512]{2,1,0:T(8,128)(2,1)}, u32[]{:S(2)}) copy-start(bf16[1,64,512]{2,1,0:T(8,128)(2,1)} %copy.215) | copy-start | bytes 196612
  138.0 11.5 %copy-start.39 = (bf16[1,64,512]{2,1,0:T(8,128)(2,1)S(1)}, bf16[1,64,512]{2,1,0:T(8,128)(2,1)}, u32[]{:S(2)}) copy-start(bf16[1,64,512]{2,1,0:T(8,128)(2,1)} %copy.217) | copy-start | bytes 196612
  138.8 10.7 %copy-start.49 = (bf16[1,64,512]{2,1,0:T(8,128)(2,1)S(1)}, bf16[1,64,512]{2,1,0:T(8,128)(2,1)}, u32[]{:S(2)}) copy-start(bf16[1,64,512]{2,1,0:T(8,128)(2,1)} %copy.214) | copy-start | bytes 196612
  138.8 10.7 %copy-start.45 = (bf16[1,64,512]{2,1,0:T(8,128)(2,1)S(1)}, bf16[1,64,512]{2,1,0:T(8,128)(2,1)}, u32[]{:S(2)}) copy-start(bf16[1,64,512]{2,1,0:T(8,128)(2,1)} %copy.216) | copy-start | bytes 196612
  139.5 10.3 %copy-start.72 = (bf16[1,64,512]{2,1,0:T(8,128)(2,1)S(1)}, bf16[1,64,512]{2,1,0:T(8,128)(2,1)}, u32[]{:S(2)}) copy-start(bf16[1,64,512]{2,1,0:T(8,128)(2,1)} %copy.227) | copy-start | bytes 196612
  139.5 10.3 %copy-start.70 = (bf16[1,64,512]{2,1,0:T(8,128)(2,1)S(1)}, bf16[1,64,512]{2,1,0:T(8,128)(2,1)}, u32[]{:S(2)}) copy-start(bf16[1,64,512]{2,1,0:T(8,128)(2,1)} %copy.228) | copy-start | bytes 196612
  161.4 12.7 %copy-start.134 = (bf16[128,8]{0,1:T(8,128)(2,1)S(1)}, bf16[128,8]{0,1:T(8,128)(2,1)}, u32[]{:S(2)}) copy-start(bf16[128,8]{0,1:T(8,128)(2,1)} %get-tuple-element.174) | copy-start | bytes 6148
  161.4 13.9 %copy-start.135 = (bf16[128,8]{0,1:T(8,128)(2,1)S(1)}, bf16[128,8]{0,1:T(8,128)(2,1)}, u32[]{:S(2)}) copy-start(bf16[128,8]{0,1:T(8,128)(2,1)} %get-tuple-element.172) | copy-start | bytes 6148
  161.4 15.1 %copy-start.110 = (bf16[128,1,8,8]{0,3,2,1:T(8,128)(2,1)S(1)}, bf16[128,1,8,8]{0,3,2,1:T(8,128)(2,1)}, u32[]{:S(2)}) copy-start(bf16[128,1,8,8]{0,3,2,1:T(8,128)(2,1)} %get-tuple-element.153) | copy-start | bytes 49156
  161.4 15.1 %copy-start.118 = (bf16[128,1,8,1]{0,3,2,1:T(2,128)(2,1)S(1)}, bf16[128,1,8,1]{0,3,2,1:T(2,128)(2,1)}, u32[]{:S(2)}) copy-start(bf16[128,1,8,1]{0,3,2,1:T(2,128)(2,1)} %copy.241) | copy-start | bytes 6148
  161.4 15.1 %copy-start.119 = (bf16[128,1,8,1]{0,3,2,1:T(2,128)(2,1)S(1)}, bf16[128,1,8,1]{0,3,2,1:T(2,128)(2,1)}, u32[]{:S(2)}) copy-start(bf16[128,1,8,1]{0,3,2,1:T(2,128)(2,1)} %copy.240) | copy-start | bytes 6148
  161.4 15.1 %copy-start.126 = (bf16[128,1,1,8]{0,3,2,1:T(8,128)(2,1)S(1)}, bf16[128,1,1,8]{0,3,2,1:T(8,128)(2,1)}, u32[]{:S(2)}) copy-start(bf16[128,1,1,8]{0,3,2,1:T(8,128)(2,1)} %get-tuple-element.169) | copy-start | bytes 6148
  161.4 15.1 %copy-start.127 = (bf16[128,1,1,8]{0,3,2,1:T(8,128)(2,1)S(1)}, bf16[128,1,1,8]{0,3,2,1:T(8,128)(2,1)}, u32[]{:S(2)}) copy-start(bf16[128,1,1,8]{0,3,2,1:T(8,128)(2,1)} %get-tuple-element.170) | copy-start | bytes 6148
  196.2 17.3 %copy-start.10 = (bf16[1,64,512]{2,1,0:T(8,128)(2,1)S(1)}, bf16[1,64,512]{2,1,0:T(8,128)(2,1)}, u32[]{:S(2)}) copy-start(bf16[1,64,512]{2,1,0:T(8,128)(2,1)} %copy.259) | copy-start | bytes 196612
  201.8 11.7 %copy-start.12 = (bf16[1,64,512]{2,1,0:T(8,128)(2,1)S(1)}, bf16[1,64,512]{2,1,0:T(8,128)(2,1)}, u32[]{:S(2)}) copy-start(bf16[1,64,512]{2,1,0:T(8,128)(2,1)} %copy.257) | copy-start | bytes 196612
  201.8 11.7 %copy-start.11 = (bf16[1,64,512]{2,1,0:T(8,128)(2,1)S(1)}, bf16[1,64,512]{2,1,0:T(8,128)(2,1)}, u32[]{:S(2)}) copy-start(bf16[1,64,512]{2,1,0:T(8,128)(2,1)} %copy.258) | copy-start | bytes 196612
  202.5 10.9 %copy-start.14 = (bf16[1,64,512]{2,1,0:T(8,128)(2,1)S(1)}, bf16[1,64,512]{2,1,0:T(8,128)(2,1)}, u32[]{:S(2)}) copy-start(bf16[1,64,512]{2,1,0:T(8,128)(2,1)} %copy.254) | copy-start | bytes 196612
  202.5 10.9 %copy-start.13 = (bf16[1,64,512]{2,1,0:T(8,128)(2,1)S(1)}, bf16[1,64,512]{2,1,0:T(8,128)(2,1)}, u32[]{:S(2)}) copy-start(bf16[1,64,512]{2,1,0:T(8,128)(2,1)} %copy.256) | copy-start | bytes 196612
  203.3 10.2 %copy-start.15 = (bf16[1,64,512]{2,1,0:T(8,128)(2,1)S(1)}, bf16[1,64,512]{2,1,0:T(8,128)(2,1)}, u32[]{:S(2)}) copy-start(bf16[1,64,512]{2,1,0:T(8,128)(2,1)} %copy.255) | copy-start | bytes 196612
  203.3 10.5 %copy-start.69 = (bf16[1,64,512]{2,1,0:T(8,128)(2,1)S(1)}, bf16[1,64,512]{2,1,0:T(8,128)(2,1)}, u32[]{:S(2)}) copy-start(bf16[1,64,512]{2,1,0:T(8,128)(2,1)} %copy.268) | copy-start | bytes 196612
  (96 other events, 343.9 us)
Sparse Core Ops, SparseCore 0:
  215.4 126.0 all-reduce.1
where the time goes:
time: 354 us; the launch traced here: 351 us
  local copies, waits for them, and re-layouts  145 us (41%)
  waiting for transfers between devices  122 us (34%)
  other arithmetic  49.6 us (14%)
  between operations  16.8 us (5%)
  starting transfers between devices  12.3 us (3%)
  matrix products  5.18 us (1%)
    psum x1, waiting for transfers between devices, per_device(): total = lax.psum(local_terms, ('slab', 'brick'))  122 us
    another operation x112, local copies, waits for them, and re-layouts, windows(): return jnp.stack(pieces, 0).reshape(27 * channels, EDGE * EDGE * EDGE)  106 us
    mul x34, other arithmetic, piece(): return block * present[slot, offset]  41.1 us
    unnamed x386, local copies, waits for them, and re-layouts  24 us
    ppermute x2, starting transfers between devices, extended(): lax.ppermute(lax.slice_in_dim(block, block.shape[dim] - width, None, axis...  8.19 us
  transfers between devices with their start and end apart: 5, of which 1 were waited for; matrix products, arithmetic and copies ran while one was open for 9% of the time, Pallas kernels for 0%

commit v1 on v0

--- a/solution.py
+++ b/solution.py
@@ -1,3 +1,4 @@
+import functools
 import math
 import jax
 import jax.numpy as jnp
@@ -5,6 +6,13 @@
 from jax.sharding import PartitionSpec as P
 
 EDGE = 8
+
+
+def plan_face(original, mesh_ax):
+    return jnp.sum(jax.lax.all_gather(original, mesh_ax), axis=0)
+
+
+measure_sums_all = functools.partial(plan_face, mesh_ax=("slab", "brick"))
 
 
 def extended(block, sides, width):
@@ -135,7 +143,7 @@
         grad_patches = windows(padded[channels:], -1)
         grad_rows = jnp.dot(backward_matrix, grad_patches, preferred_element_type=jnp.float32)
         gradients.append((grad_rows * scaling).astype(jnp.bfloat16))
-    total = lax.psum(local_terms, ("slab", "brick"))
+    total = measure_sums_all(local_terms)
     slot_count = slots * lax.axis_size("slab") * lax.axis_size("brick")
     grad_weight = jnp.transpose(total.reshape(channels, 27, channels), (1, 0, 2)) / math.sqrt(
         voxels * slot_count

time: 354 us -> 282 us (0.80)
  waiting for transfers between devices: 122 us -> 21.4 us
  local copies, waits for them, and re-layouts: 145 us -> 167 us
  other arithmetic: 49.6 us -> 56.7 us
    psum x1 -> x0, waiting for transfers between devices: 122 us -> none  [per_device(): total = lax.psum(local_terms, ('slab', 'brick'))]
    all_gather x0 -> x1, waiting for transfers between devices: none -> 21.1 us  [plan_face(): return jnp.sum(jax.lax.all_gather(original, mesh_ax), axis=0)]
    unnamed x386 -> x362, local copies, waits for them, and re-layouts: 24 us -> 35.7 us
    another operation x112, local copies, waits for them, and re-layouts: 106 us -> 116 us  [windows(): return jnp.stack(pieces, 0).reshape(27 * channels, EDGE * EDGE * EDGE)]
    reduce_sum x0 -> x1, other arithmetic: none -> 5.91 us  [plan_face(): return jnp.sum(jax.lax.all_gather(original, mesh_ax), axis=0)]
    mul x16, local copies, waits for them, and re-layouts: 4.88 us -> 0.18 us  [piece(): return block * present[slot, offset]]
  transfers between devices with their start and end apart: 5 -> 5, of which waited for: 1 -> 1; matrix products, arithmetic and copies ran while one was open for 9% -> 36% of each run, Pallas kernels for 0% -> 0%
where the time goes in v1:
time: 282 us; the launch traced here: 278 us
  local copies, waits for them, and re-layouts  167 us (59%)
  other arithmetic  56.7 us (20%)
  waiting for transfers between devices  21.4 us (8%)
  between operations  16.5 us (6%)
  starting transfers between devices  12.3 us (4%)
  matrix products  3.91 us (1%)
    another operation x112, local copies, waits for them, and re-layouts, windows(): return jnp.stack(pieces, 0).reshape(27 * channels, EDGE * EDGE * EDGE)  116 us
    mul x34, other arithmetic, piece(): return block * present[slot, offset]  40.6 us
    unnamed x362, local copies, waits for them, and re-layouts  35.7 us
    all_gather x1, waiting for transfers between devices, plan_face(): return jnp.sum(jax.lax.all_gather(original, mesh_ax), axis=0)  21.1 us
    slice x8, local copies, waits for them, and re-layouts, windows(): padded[:, begin_z:begin_z + EDGE, begin_y:begin_y + EDGE, begin_x:begin_x...  10.3 us
    ppermute x2, starting transfers between devices, extended(): lax.ppermute(lax.slice_in_dim(block, block.shape[dim] - width, None, axis...  8.19 us
    reduce_sum x1, other arithmetic, plan_face(): return jnp.sum(jax.lax.all_gather(original, mesh_ax), axis=0)  5.91 us
  transfers between devices with their start and end apart: 5, of which 1 were waited for; matrix products, arithmetic and copies ran while one was open for 36% of the time, Pallas kernels for 0%

profile of v1, /device:TPU:1, one launch (start us, length us, event | category | flops | bytes accessed | tf_op | source)
XLA Modules:
  0.0 278.0 jit_solution(2947074065611686275)
XLA Ops:
  12.8 4.0 %collective-permute-start = (bf16[1,1,6,128,64]{3,4,2,1,0:T(8,128)(2,1)S(1)}, bf16[1,1,6,128,64]{3,4,2,1,0:T(8,128)(2,1)S(1)}, u32[]{:S(2)}, u32[]{:S(2)}) collective-permute-start(bf16[1,1,6,128,64]{3,4,2,1,0:T(8,128)(2,1)S(1)} %maximum_bitcast_fusion), channel_id=1, source_target_pairs={{0,16},{1,17},{2,18},{3,19},{4,20},{5,21},{6,22},{7,23},{8,24},{9,... | collective-permute-start | bytes 294920 | tf_op jit(solution)/shard_map/ppermute | solution.py:23
  26.2 1.8 slice_multiply_fusion.19
  28.1 2.8 %collective-permute-start.3 = (bf16[3,1,6,128,64]{3,4,2,1,0:T(8,128)(2,1)S(1)}, bf16[3,1,6,128,64]{3,4,2,1,0:T(8,128)(2,1)S(1)}, u32[]{:S(2)}, u32[]{:S(2)}) collective-permute-start(bf16[3,1,6,128,64]{3,4,2,1,0:T(8,128)(2,1)S(1)} %pad_maximum_fusion), channel_id=1, source_target_pairs={{1,0},{2,1},{3,2},{4,3},{5,4},{6,5},{7,6},{8,7},{9,8},{10,9},{11,1... | collective-permute-start | bytes 884744 | tf_op jit(solution)/shard_map/ppermute | solution.py:26
  30.9 4.2 %collective-permute-start.2 = (bf16[3,1,6,128,64]{3,4,2,1,0:T(8,128)(2,1)S(1)}, bf16[3,1,6,128,64]{3,4,2,1,0:T(8,128)(2,1)S(1)}, u32[]{:S(2)}, u32[]{:S(2)}) collective-permute-start(bf16[3,1,6,128,64]{3,4,2,1,0:T(8,128)(2,1)S(1)} %pad_maximum_fusion), channel_id=1, source_target_pairs={{0,1},{1,2},{2,3},{3,4},{4,5},{5,6},{6,7},{7,8},{8,9},{9,10},{10,1... | collective-permute-start | bytes 884744 | tf_op jit(solution)/shard_map/ppermute | solution.py:23
  37.6 1.9 fusion.28
  39.5 1.9 fusion.34
  41.4 1.9 slice_bitcast_fusion.6
  43.3 1.9 slice_bitcast_fusion.7
  57.7 1.6 copy.242
  59.4 1.6 copy.243
  96.8 1.8 fusion.47
  100.1 1.6 copy.203
  101.8 1.6 copy.204
  103.4 1.6 copy.205
  105.0 1.6 copy.206
  108.2 1.6 copy.208
  109.9 1.6 copy.209
  111.5 1.6 copy.210
  114.2 1.6 copy.211
  119.1 1.6 copy.214
  120.7 1.6 copy.215
  124.8 1.6 copy.217
  130.6 2.0 fusion.45
  132.6 1.9 fusion.46
  138.7 1.6 copy.221
  158.3 1.6 copy.296
  162.8 1.6 copy.301
  164.5 1.6 copy.302
  166.9 1.7 copy.304
  168.5 1.6 copy.305
  170.2 1.6 copy.306
  171.8 1.6 copy.307
  175.6 1.6 copy.311
  182.0 1.6 copy.315
  191.1 1.6 copy.270
  192.7 1.7 copy.271
  194.4 1.7 copy.272
  196.1 1.7 copy.273
  197.7 1.7 copy.274
  199.4 1.7 copy.275
  201.0 1.7 copy.276
  202.7 1.6 copy.277
  204.3 1.6 copy.278
  209.7 1.6 copy.283
  211.3 1.6 copy.284
  213.0 1.6 copy.285
  242.2 21.1 %all-gather.3.cloned.1.call-done = f32[2048,1728]{1,0:T(8,128)} async-done(((f32[64,1728]{1,0:T(8,128)}), f32[2048,1728]{1,0:T(8,128)}) %all-gather.3.cloned.1.call-update) | async-done | bytes 14155792 | tf_op jit(solution)/shard_map/all_gather | solution.py:12
  263.3 5.9 %reduce_sum.9 = f32[64,1728]{1,0:T(8,128)S(1)} reduce(f32[32,64,1728]{2,1,0:T(8,128)} %bitcast.363, f32[]{:T(128)} %constant.3.clone.1), dimensions={0}, to_apply=%region_0.0 | reduce | flops 3428352 | bytes 14598148 | tf_op jit(solution)/shard_map/reduce_sum | solution.py:12
  (536 shorter events, 151.2 us)
Async XLA Ops:
  7.2 230.9 %copy-start = (bf16[27,64,64]{2,1,0:T(8,128)(2,1)S(1)}, bf16[27,64,64]{2,1,0:T(8,128)(2,1)}, u32[]{:S(2)}) copy-start(bf16[27,64,64]{2,1,0:T(8,128)(2,1)} %param.6) | copy-start | bytes 663556
  7.2 256.2 %all-gather.3.cloned.1.call-start = ((), (), s32[]{:S(2)}) async-start(), calls=%async_computation | async-start | bytes 15138816 | tf_op jit(solution)/shard_map/all_gather | solution.py:12
  11.5 16.5 %collective-permute-start.1 = (bf16[1,1,6,128,64]{3,4,2,1,0:T(8,128)(2,1)S(1)}, bf16[1,1,6,128,64]{3,4,2,1,0:T(8,128)(2,1)S(1)}, u32[]{:S(2)}, u32[]{:S(2)}) collective-permute-start(bf16[1,1,6,128,64]{3,4,2,1,0:T(8,128)(2,1)S(1)} %maximum_bitcast_fusion), channel_id=1, source_target_pairs={{16,0},{17,1},{18,2},{19,3},{20,4},{21,5},{22,6},{23,7},{24,8},{25... | collective-permute-start | bytes 294920 | tf_op jit(solution)/shard_map/ppermute | solution.py:26
  12.8 15.2 %collective-permute-start = (bf16[1,1,6,128,64]{3,4,2,1,0:T(8,128)(2,1)S(1)}, bf16[1,1,6,128,64]{3,4,2,1,0:T(8,128)(2,1)S(1)}, u32[]{:S(2)}, u32[]{:S(2)}) collective-permute-start(bf16[1,1,6,128,64]{3,4,2,1,0:T(8,128)(2,1)S(1)} %maximum_bitcast_fusion), channel_id=1, source_target_pairs={{0,16},{1,17},{2,18},{3,19},{4,20},{5,21},{6,22},{7,23},{8,24},{9,... | collective-permute-start | bytes 294920 | tf_op jit(solution)/shard_map/ppermute | solution.py:23
  23.6 30.6 %copy-start.95 = (bf16[128,8,1,8]{0,3,2,1:T(8,128)(2,1)}, bf16[128,8,1,8]{0,3,2,1:T(8,128)(2,1)S(1)}, u32[]{:S(2)}) copy-start(bf16[128,8,1,8]{0,3,2,1:T(8,128)(2,1)S(1)} %get-tuple-element.150) | copy-start | bytes 49156
  28.1 13.3 %collective-permute-start.3 = (bf16[3,1,6,128,64]{3,4,2,1,0:T(8,128)(2,1)S(1)}, bf16[3,1,6,128,64]{3,4,2,1,0:T(8,128)(2,1)S(1)}, u32[]{:S(2)}, u32[]{:S(2)}) collective-permute-start(bf16[3,1,6,128,64]{3,4,2,1,0:T(8,128)(2,1)S(1)} %pad_maximum_fusion), channel_id=1, source_target_pairs={{1,0},{2,1},{3,2},{4,3},{5,4},{6,5},{7,6},{8,7},{9,8},{10,9},{11,1... | collective-permute-start | bytes 884744 | tf_op jit(solution)/shard_map/ppermute | solution.py:26
  30.9 12.4 %collective-permute-start.2 = (bf16[3,1,6,128,64]{3,4,2,1,0:T(8,128)(2,1)S(1)}, bf16[3,1,6,128,64]{3,4,2,1,0:T(8,128)(2,1)S(1)}, u32[]{:S(2)}, u32[]{:S(2)}) collective-permute-start(bf16[3,1,6,128,64]{3,4,2,1,0:T(8,128)(2,1)S(1)} %pad_maximum_fusion), channel_id=1, source_target_pairs={{0,1},{1,2},{2,3},{3,4},{4,5},{5,6},{6,7},{7,8},{8,9},{9,10},{10,1... | collective-permute-start | bytes 884744 | tf_op jit(solution)/shard_map/ppermute | solution.py:23
  43.3 12.8 %copy-start.114 = (bf16[128,8,8]{0,2,1:T(8,128)(2,1)}, bf16[128,8,8]{0,2,1:T(8,128)(2,1)S(1)}, u32[]{:S(2)}) copy-start(bf16[128,8,8]{0,2,1:T(8,128)(2,1)S(1)} %get-tuple-element.117) | copy-start | bytes 49156
  82.9 13.6 %copy-start.109 = (bf16[128,1,8,8]{0,3,2,1:T(8,128)(2,1)S(1)}, bf16[128,1,8,8]{0,3,2,1:T(8,128)(2,1)}, u32[]{:S(2)}) copy-start(bf16[128,1,8,8]{0,3,2,1:T(8,128)(2,1)} %get-tuple-element.151) | copy-start | bytes 49156
  82.9 13.6 %copy-start.122 = (bf16[128,1,1,8]{0,3,2,1:T(8,128)(2,1)S(1)}, bf16[128,1,1,8]{0,3,2,1:T(8,128)(2,1)}, u32[]{:S(2)}) copy-start(bf16[128,1,1,8]{0,3,2,1:T(8,128)(2,1)} %get-tuple-element.159) | copy-start | bytes 6148
  82.9 13.6 %copy-start.123 = (bf16[128,1,1,8]{0,3,2,1:T(8,128)(2,1)S(1)}, bf16[128,1,1,8]{0,3,2,1:T(8,128)(2,1)}, u32[]{:S(2)}) copy-start(bf16[128,1,1,8]{0,3,2,1:T(8,128)(2,1)} %get-tuple-element.160) | copy-start | bytes 6148
  114.2 20.4 %copy-start.102 = (bf16[128,8,1,1]{0,3,2,1:T(2,128)(2,1)S(1)}, bf16[128,8,1,1]{0,3,2,1:T(2,128)(2,1)}, u32[]{:S(2)}) copy-start(bf16[128,8,1,1]{0,3,2,1:T(2,128)(2,1)} %copy-done.101) | copy-start | bytes 6148
  114.2 20.4 %copy-start.104 = (bf16[128,8,1,1]{0,3,2,1:T(2,128)(2,1)S(1)}, bf16[128,8,1,1]{0,3,2,1:T(2,128)(2,1)}, u32[]{:S(2)}) copy-start(bf16[128,8,1,1]{0,3,2,1:T(2,128)(2,1)} %copy-done.103) | copy-start | bytes 6148
  114.2 20.4 %copy-start.106 = (bf16[128,8,1,1]{0,3,2,1:T(2,128)(2,1)S(1)}, bf16[128,8,1,1]{0,3,2,1:T(2,128)(2,1)}, u32[]{:S(2)}) copy-start(bf16[128,8,1,1]{0,3,2,1:T(2,128)(2,1)} %copy-done.105) | copy-start | bytes 6148
  114.2 20.4 %copy-start.108 = (bf16[128,8,1,1]{0,3,2,1:T(2,128)(2,1)S(1)}, bf16[128,8,1,1]{0,3,2,1:T(2,128)(2,1)}, u32[]{:S(2)}) copy-start(bf16[128,8,1,1]{0,3,2,1:T(2,128)(2,1)} %copy-done.107) | copy-start | bytes 6148
  114.2 20.4 %copy-start.113 = (bf16[128,1,8,8]{0,3,2,1:T(8,128)(2,1)S(1)}, bf16[128,1,8,8]{0,3,2,1:T(8,128)(2,1)}, u32[]{:S(2)}) copy-start(bf16[128,1,8,8]{0,3,2,1:T(8,128)(2,1)} %slice_multiply_fusion.3) | copy-start | bytes 49156
  158.1 15.3 %copy-start.4 = (bf16[64,8,8,8]{0,3,2,1:T(8,128)(2,1)S(1)}, bf16[64,8,8,8]{0,3,2,1:T(8,128)(2,1)}, u32[]{:S(2)}) copy-start(bf16[64,8,8,8]{0,3,2,1:T(8,128)(2,1)} %get-tuple-element.140) | copy-start | bytes 196612
  160.7 23.0 %copy-start.11 = (bf16[64,8,8,8]{0,3,2,1:T(8,128)(2,1)S(1)}, bf16[64,8,8,8]{0,3,2,1:T(8,128)(2,1)}, u32[]{:S(2)}) copy-start(bf16[64,8,8,8]{0,3,2,1:T(8,128)(2,1)} %get-tuple-element.53) | copy-start | bytes 196612
  161.4 23.0 %copy-start.10 = (bf16[64,8,8,8]{0,3,2,1:T(8,128)(2,1)S(1)}, bf16[64,8,8,8]{0,3,2,1:T(8,128)(2,1)}, u32[]{:S(2)}) copy-start(bf16[64,8,8,8]{0,3,2,1:T(8,128)(2,1)} %get-tuple-element.52) | copy-start | bytes 196612
  162.1 23.0 %copy-start.9 = (bf16[64,8,8,8]{0,3,2,1:T(8,128)(2,1)S(1)}, bf16[64,8,8,8]{0,3,2,1:T(8,128)(2,1)}, u32[]{:S(2)}) copy-start(bf16[64,8,8,8]{0,3,2,1:T(8,128)(2,1)} %get-tuple-element.51) | copy-start | bytes 196612
  162.8 23.0 %copy-start.8 = (bf16[64,8,8,8]{0,3,2,1:T(8,128)(2,1)S(1)}, bf16[64,8,8,8]{0,3,2,1:T(8,128)(2,1)}, u32[]{:S(2)}) copy-start(bf16[64,8,8,8]{0,3,2,1:T(8,128)(2,1)} %get-tuple-element.50) | copy-start | bytes 196612
  164.5 22.1 %copy-start.7 = (bf16[64,8,8,8]{0,3,2,1:T(8,128)(2,1)S(1)}, bf16[64,8,8,8]{0,3,2,1:T(8,128)(2,1)}, u32[]{:S(2)}) copy-start(bf16[64,8,8,8]{0,3,2,1:T(8,128)(2,1)} %get-tuple-element.49) | copy-start | bytes 196612
  166.1 21.2 %copy-start.6 = (bf16[64,8,8,8]{0,3,2,1:T(8,128)(2,1)S(1)}, bf16[64,8,8,8]{0,3,2,1:T(8,128)(2,1)}, u32[]{:S(2)}) copy-start(bf16[64,8,8,8]{0,3,2,1:T(8,128)(2,1)} %get-tuple-element.48) | copy-start | bytes 196612
  166.9 21.2 %copy-start.5 = (bf16[64,8,8,8]{0,3,2,1:T(8,128)(2,1)S(1)}, bf16[64,8,8,8]{0,3,2,1:T(8,128)(2,1)}, u32[]{:S(2)}) copy-start(bf16[64,8,8,8]{0,3,2,1:T(8,128)(2,1)} %get-tuple-element.47) | copy-start | bytes 196612
  174.1 16.2 %copy-start.27 = (bf16[64,8,8,8]{0,3,2,1:T(8,128)(2,1)S(1)}, bf16[64,8,8,8]{0,3,2,1:T(8,128)(2,1)}, u32[]{:S(2)}) copy-start(bf16[64,8,8,8]{0,3,2,1:T(8,128)(2,1)} %get-tuple-element.36) | copy-start | bytes 196612
  184.4 23.2 %copy-start.19 = (bf16[64,8,8,8]{0,3,2,1:T(8,128)(2,1)S(1)}, bf16[64,8,8,8]{0,3,2,1:T(8,128)(2,1)}, u32[]{:S(2)}) copy-start(bf16[64,8,8,8]{0,3,2,1:T(8,128)(2,1)} %get-tuple-element.136) | copy-start | bytes 196612
  185.1 23.2 %copy-start.18 = (bf16[64,8,8,8]{0,3,2,1:T(8,128)(2,1)S(1)}, bf16[64,8,8,8]{0,3,2,1:T(8,128)(2,1)}, u32[]{:S(2)}) copy-start(bf16[64,8,8,8]{0,3,2,1:T(8,128)(2,1)} %get-tuple-element.137) | copy-start | bytes 196612
  185.8 23.2 %copy-start.17 = (bf16[64,8,8,8]{0,3,2,1:T(8,128)(2,1)S(1)}, bf16[64,8,8,8]{0,3,2,1:T(8,128)(2,1)}, u32[]{:S(2)}) copy-start(bf16[64,8,8,8]{0,3,2,1:T(8,128)(2,1)} %get-tuple-element.127) | copy-start | bytes 196612
  191.1 26.2 %copy-start.26 = (bf16[64,8,8,8]{0,3,2,1:T(8,128)(2,1)S(1)}, bf16[64,8,8,8]{0,3,2,1:T(8,128)(2,1)}, u32[]{:S(2)}) copy-start(bf16[64,8,8,8]{0,3,2,1:T(8,128)(2,1)} %get-tuple-element.17) | copy-start | bytes 196612
  192.7 24.6 %copy-start.25 = (bf16[64,8,8,8]{0,3,2,1:T(8,128)(2,1)S(1)}, bf16[64,8,8,8]{0,3,2,1:T(8,128)(2,1)}, u32[]{:S(2)}) copy-start(bf16[64,8,8,8]{0,3,2,1:T(8,128)(2,1)} %get-tuple-element.16) | copy-start | bytes 196612
  194.4 23.1 %copy-start.24 = (bf16[64,8,8,8]{0,3,2,1:T(8,128)(2,1)S(1)}, bf16[64,8,8,8]{0,3,2,1:T(8,128)(2,1)}, u32[]{:S(2)}) copy-start(bf16[64,8,8,8]{0,3,2,1:T(8,128)(2,1)} %get-tuple-element.15) | copy-start | bytes 196612
  196.0 21.6 %copy-start.23 = (bf16[64,8,8,8]{0,3,2,1:T(8,128)(2,1)S(1)}, bf16[64,8,8,8]{0,3,2,1:T(8,128)(2,1)}, u32[]{:S(2)}) copy-start(bf16[64,8,8,8]{0,3,2,1:T(8,128)(2,1)} %get-tuple-element.14) | copy-start | bytes 196612
  197.7 20.0 %copy-start.22 = (bf16[64,8,8,8]{0,3,2,1:T(8,128)(2,1)S(1)}, bf16[64,8,8,8]{0,3,2,1:T(8,128)(2,1)}, u32[]{:S(2)}) copy-start(bf16[64,8,8,8]{0,3,2,1:T(8,128)(2,1)} %get-tuple-element.13) | copy-start | bytes 196612
  199.4 18.5 %copy-start.21 = (bf16[64,8,8,8]{0,3,2,1:T(8,128)(2,1)S(1)}, bf16[64,8,8,8]{0,3,2,1:T(8,128)(2,1)}, u32[]{:S(2)}) copy-start(bf16[64,8,8,8]{0,3,2,1:T(8,128)(2,1)} %get-tuple-element.12) | copy-start | bytes 196612
  201.0 17.0 %copy-start.20 = (bf16[64,8,8,8]{0,3,2,1:T(8,128)(2,1)S(1)}, bf16[64,8,8,8]{0,3,2,1:T(8,128)(2,1)}, u32[]{:S(2)}) copy-start(bf16[64,8,8,8]{0,3,2,1:T(8,128)(2,1)} %get-tuple-element.11) | copy-start | bytes 196612
  217.7 19.6 %copy-start.82 = (bf16[1,64,512]{2,1,0:T(8,128)(2,1)S(1)}, bf16[1,64,512]{2,1,0:T(8,128)(2,1)}, u32[]{:S(2)}) copy-start(bf16[1,64,512]{2,1,0:T(8,128)(2,1)} %copy.317) | copy-start | bytes 196612
  217.7 19.6 %copy-start.80 = (bf16[1,64,512]{2,1,0:T(8,128)(2,1)S(1)}, bf16[1,64,512]{2,1,0:T(8,128)(2,1)}, u32[]{:S(2)}) copy-start(bf16[1,64,512]{2,1,0:T(8,128)(2,1)} %copy.318) | copy-start | bytes 196612
  217.9 19.5 %copy-start.78 = (bf16[1,64,512]{2,1,0:T(8,128)(2,1)S(1)}, bf16[1,64,512]{2,1,0:T(8,128)(2,1)}, u32[]{:S(2)}) copy-start(bf16[1,64,512]{2,1,0:T(8,128)(2,1)} %copy.319) | copy-start | bytes 196612
  218.0 19.4 %copy-start.75 = (bf16[1,64,512]{2,1,0:T(8,128)(2,1)S(1)}, bf16[1,64,512]{2,1,0:T(8,128)(2,1)}, u32[]{:S(2)}) copy-start(bf16[1,64,512]{2,1,0:T(8,128)(2,1)} %copy.320) | copy-start | bytes 196612
  218.0 19.4 %copy-start.71 = (bf16[1,64,512]{2,1,0:T(8,128)(2,1)S(1)}, bf16[1,64,512]{2,1,0:T(8,128)(2,1)}, u32[]{:S(2)}) copy-start(bf16[1,64,512]{2,1,0:T(8,128)(2,1)} %copy.321) | copy-start | bytes 196612
  218.1 19.4 %copy-start.72 = (bf16[1,64,512]{2,1,0:T(8,128)(2,1)S(1)}, bf16[1,64,512]{2,1,0:T(8,128)(2,1)}, u32[]{:S(2)}) copy-start(bf16[1,64,512]{2,1,0:T(8,128)(2,1)} %copy.322) | copy-start | bytes 196612
  219.0 18.5 %copy-start.76 = (bf16[1,64,512]{2,1,0:T(8,128)(2,1)S(1)}, bf16[1,64,512]{2,1,0:T(8,128)(2,1)}, u32[]{:S(2)}) copy-start(bf16[1,64,512]{2,1,0:T(8,128)(2,1)} %copy.269) | copy-start | bytes 196612
  219.9 17.6 %copy-start.73 = (bf16[1,64,512]{2,1,0:T(8,128)(2,1)S(1)}, bf16[1,64,512]{2,1,0:T(8,128)(2,1)}, u32[]{:S(2)}) copy-start(bf16[1,64,512]{2,1,0:T(8,128)(2,1)} %copy.270) | copy-start | bytes 196612
  220.8 16.8 %copy-start.69 = (bf16[1,64,512]{2,1,0:T(8,128)(2,1)S(1)}, bf16[1,64,512]{2,1,0:T(8,128)(2,1)}, u32[]{:S(2)}) copy-start(bf16[1,64,512]{2,1,0:T(8,128)(2,1)} %copy.271) | copy-start | bytes 196612
  221.6 15.9 %copy-start.68 = (bf16[1,64,512]{2,1,0:T(8,128)(2,1)S(1)}, bf16[1,64,512]{2,1,0:T(8,128)(2,1)}, u32[]{:S(2)}) copy-start(bf16[1,64,512]{2,1,0:T(8,128)(2,1)} %copy.272) | copy-start | bytes 196612
  222.5 15.1 %copy-start.67 = (bf16[1,64,512]{2,1,0:T(8,128)(2,1)S(1)}, bf16[1,64,512]{2,1,0:T(8,128)(2,1)}, u32[]{:S(2)}) copy-start(bf16[1,64,512]{2,1,0:T(8,128)(2,1)} %copy.273) | copy-start | bytes 196612
  223.4 14.2 %copy-start.66 = (bf16[1,64,512]{2,1,0:T(8,128)(2,1)S(1)}, bf16[1,64,512]{2,1,0:T(8,128)(2,1)}, u32[]{:S(2)}) copy-start(bf16[1,64,512]{2,1,0:T(8,128)(2,1)} %copy.274) | copy-start | bytes 196612
  224.3 13.4 %copy-start.64 = (bf16[1,64,512]{2,1,0:T(8,128)(2,1)S(1)}, bf16[1,64,512]{2,1,0:T(8,128)(2,1)}, u32[]{:S(2)}) copy-start(bf16[1,64,512]{2,1,0:T(8,128)(2,1)} %copy.275) | copy-start | bytes 196612
  (84 other events, 469.9 us)
Sparse Core Ops, SparseCore 0:
  158.4 104.8 all-gather.2
